TPU v7x, 512 devices: a whole 4x4x16 slice. The times are simulated.
512 devices in a mesh: term: 32 (over y, x, core), sector: 16 (over z).
Axes of the slice: x: 4, y: 4, z: 16, core: 2. Of those that a mesh axis runs over, the one named last changes fastest.
Arguments:
- wavefunction: bfloat16 [96, 256, 256], P('sector')
- left_operator_blocks: bfloat16 [384, 256, 256], P('term'), may hold values from -0.01953125 to 0.01953125
- right_operator_blocks: bfloat16 [384, 256, 256], P('term'), may hold values from -0.375 to 0.375
- fetch_index: int32 [32, 16, 16], P('term', 'sector'), may hold values from 0 to 5, as said below
- owner_link: int32 [384, 96], P('term', 'sector'), may hold values from 0 to 15, as said below
- lower_roots: bfloat16 [4, 96, 256, 256], P(None, 'sector', 'term')
- level_shift: float32 [4], replicated, may hold values from 0.5 to 2
Outputs:
- sigma: float32 [96, 256, 256], P('sector', 'term')
- correlations: float32 [4], replicated
Inputs may be any that keep to these rules, and one draw needn't show every extreme that they name: `fetch_index`: entry p of every list is a position within the 6 sectors of sector index p. `owner_link`: within the 12 x 6 entries that one device holds, every sector index occurs at least once.
All inputs are finite; a program needn't handle non-finite values.
Results may differ from a plain program's by a relative error of at most 0.0059.
Values may be sent and summed in bfloat16 or wider, within the bound.
A program may use at most 64 MiB of HBM per device.

v0:
```python
import jax
import jax.numpy as jnp
from jax import lax
from jax.sharding import PartitionSpec as P


def per_device(
    wavefunction,
    left_operator_blocks,
    right_operator_blocks,
    fetch_index,
    owner_link,
    lower_roots,
    level_shift,
):
    sec_dev = wavefunction.shape[0]
    block_width = wavefunction.shape[1]
    group_count = fetch_index.shape[2]
    own_requests = fetch_index.reshape(group_count, 1)
    store = lax.all_gather(wavefunction, "sector", axis=0, tiled=True)
    lookup = owner_link * sec_dev + own_requests[:, 0][owner_link]

    def one_sector(column):
        input_sectors = store[column]
        partial_contraction = jnp.einsum(
            "lhm,lmp->lhp", left_operator_blocks, input_sectors, preferred_element_type=jnp.float32
        ).astype(jnp.bfloat16)
        return jnp.einsum(
            "yxz,ysz->xs",
            partial_contraction,
            right_operator_blocks,
            preferred_element_type=jnp.float32,
        )

    partial_value = lax.map(one_sector, jnp.transpose(lookup))
    reduced = lax.psum_scatter(partial_value, "term", scatter_dimension=1, tiled=True)
    row_count = reduced.shape[1]
    row_start = lax.axis_index("term") * row_count
    psi_rows = lax.dynamic_slice_in_dim(wavefunction, row_start, row_count, 1)
    local_correlation = jnp.einsum(
        "ksab,sab->k", lower_roots, psi_rows, preferred_element_type=jnp.float32
    )
    total_cells = lax.axis_size("sector") * sec_dev * block_width * block_width
    correlations = lax.psum(local_correlation, ("term", "sector")) / total_cells
    sigma = reduced + jnp.einsum(
        "k,ksab->sab", level_shift * correlations, lower_roots.astype(jnp.float32)
    )
    return (sigma, correlations)


def solution(mesh):
    return jax.shard_map(
        per_device,
        mesh=mesh,
        in_specs=(
            P("sector", None, None),
            P("term", None, None),
            P("term", None, None),
            P("term", "sector", None),
            P("term", "sector"),
            P(None, "sector", "term", None),
            P(),
        ),
        out_specs=(P("sector", "term", None), P()),
        check_vma=False,
    )
```

profile of v0, /device:TPU:1, one launch (start us, length us, event | category | flops | bytes accessed | tf_op | source)
XLA Modules:
  0.0 328.3 jit_solution(2077307641894323809)
XLA Ops:
  7.2 0.0 copy-start
  7.2 0.0 copy-start.1
  7.2 0.0 all-gather.2.cloned.1.call-start
  7.2 0.7 all-gather.2.cloned.1.call-update
  7.9 0.0 reduce-scatter.2.cloned.1.call-start
  8.0 0.8 copy.17
  8.8 0.7 compare_select_fusion.1
  9.4 0.1 copy.18
  9.5 0.1 reshape.42
  9.6 0.0 copy-done.1
  9.7 0.0 copy-start.2
  9.7 1.2 gather_fusion.1
  10.9 0.1 reshape.41
  11.0 0.1 copy.19
  11.1 152.4 %all-gather.2.cloned.1.call-done = bf16[96,256,256]{2,1,0:T(8,128)(2,1)} async-done(((bf16[6,256,256]{2,1,0:T(8,128)(2,1)}), bf16[96,256,256]{2,1,0:T(8,128)(2,1)}) %all-gather.2.cloned.1.call-update) | async-done | bytes 12582928 | tf_op jit(solution)/shard_map/all_gather | solution.py:20
  163.5 0.0 copy-done.2
  163.5 52.1 %while.10 = (s32[]{:T(128)}, f32[6,256,256]{2,1,0:T(8,128)}, s32[6,12]{1,0:T(8,128)S(1)}, bf16[96,256,256]{2,1,0:T(8,128)(2,1)}, bf16[12,256,256]{2,1,0:T(8,128)...) while((s32[]{:T(128)}, f32[6,256,256]{2,1,0:T(8,128)}, s32[6,12]{1,0:T(8,128)S(1)}, ...), condition=%wide.region_1.2_spmd, body=%wide.region_0.1_spmd.sunk | while | flops 806093888 | bytes 8130845 | solution.py:35
  163.5 5.2 %gather_fusion = bf16[12,256,256]{2,1,0:T(8,128)(2,1)S(1)} fusion(bf16[96,256,256]{2,1,0:T(8,128)(2,1)} %get-tuple-element.119, s32[1024]{0:T(1024)S(1)} %pad_clamp_fusion.3), kind=kCustom, calls=%fused_computation.clone.1 | custom fusion | bytes 3145776 | tf_op jit(solution)/shard_map/while/body/eval_jaxpr/gather | solution.py:24
  168.8 3.4 %fusion.27 = f32[6,256,256]{2,1,0:T(8,128)} fusion(f32[6,256,256]{2,1,0:T(8,128)} %get-tuple-element.110, s32[]{:T(128)S(6)} %copy.38, bf16[12,256,256]{2,1,0:T(8,128)(2,1)} %get-tuple-element.121, bf16[12,256,256]{2,1,0:T(8,128)(2,1)S(1)} %gather_fusion, bf16[12,256,256]{2,1,0:T(8,128)(2,1)S(1)} %get-tuple-element.120), kind=kOutput, calls=%fused_computation.6.clone.1 | convolution fusion | flops 806092800 | bytes 4980740 | tf_op jit(solution)/shard_map/while/body/eval_jaxpr/yxz,ysz->xs/dot_general | solution.py:28
  172.2 5.2 %gather_fusion = bf16[12,256,256]{2,1,0:T(8,128)(2,1)S(1)} fusion(bf16[96,256,256]{2,1,0:T(8,128)(2,1)} %get-tuple-element.119, s32[1024]{0:T(1024)S(1)} %pad_clamp_fusion.3), kind=kCustom, calls=%fused_computation.clone.1 | custom fusion | bytes 3145776 | tf_op jit(solution)/shard_map/while/body/eval_jaxpr/gather | solution.py:24
  177.4 3.5 %fusion.27 = f32[6,256,256]{2,1,0:T(8,128)} fusion(f32[6,256,256]{2,1,0:T(8,128)} %get-tuple-element.110, s32[]{:T(128)S(6)} %copy.38, bf16[12,256,256]{2,1,0:T(8,128)(2,1)} %get-tuple-element.121, bf16[12,256,256]{2,1,0:T(8,128)(2,1)S(1)} %gather_fusion, bf16[12,256,256]{2,1,0:T(8,128)(2,1)S(1)} %get-tuple-element.120), kind=kOutput, calls=%fused_computation.6.clone.1 | convolution fusion | flops 806092800 | bytes 4980740 | tf_op jit(solution)/shard_map/while/body/eval_jaxpr/yxz,ysz->xs/dot_general | solution.py:28
  180.9 5.2 %gather_fusion = bf16[12,256,256]{2,1,0:T(8,128)(2,1)S(1)} fusion(bf16[96,256,256]{2,1,0:T(8,128)(2,1)} %get-tuple-element.119, s32[1024]{0:T(1024)S(1)} %pad_clamp_fusion.3), kind=kCustom, calls=%fused_computation.clone.1 | custom fusion | bytes 3145776 | tf_op jit(solution)/shard_map/while/body/eval_jaxpr/gather | solution.py:24
  186.1 3.4 %fusion.27 = f32[6,256,256]{2,1,0:T(8,128)} fusion(f32[6,256,256]{2,1,0:T(8,128)} %get-tuple-element.110, s32[]{:T(128)S(6)} %copy.38, bf16[12,256,256]{2,1,0:T(8,128)(2,1)} %get-tuple-element.121, bf16[12,256,256]{2,1,0:T(8,128)(2,1)S(1)} %gather_fusion, bf16[12,256,256]{2,1,0:T(8,128)(2,1)S(1)} %get-tuple-element.120), kind=kOutput, calls=%fused_computation.6.clone.1 | convolution fusion | flops 806092800 | bytes 4980740 | tf_op jit(solution)/shard_map/while/body/eval_jaxpr/yxz,ysz->xs/dot_general | solution.py:28
  189.6 5.2 %gather_fusion = bf16[12,256,256]{2,1,0:T(8,128)(2,1)S(1)} fusion(bf16[96,256,256]{2,1,0:T(8,128)(2,1)} %get-tuple-element.119, s32[1024]{0:T(1024)S(1)} %pad_clamp_fusion.3), kind=kCustom, calls=%fused_computation.clone.1 | custom fusion | bytes 3145776 | tf_op jit(solution)/shard_map/while/body/eval_jaxpr/gather | solution.py:24
  194.8 3.4 %fusion.27 = f32[6,256,256]{2,1,0:T(8,128)} fusion(f32[6,256,256]{2,1,0:T(8,128)} %get-tuple-element.110, s32[]{:T(128)S(6)} %copy.38, bf16[12,256,256]{2,1,0:T(8,128)(2,1)} %get-tuple-element.121, bf16[12,256,256]{2,1,0:T(8,128)(2,1)S(1)} %gather_fusion, bf16[12,256,256]{2,1,0:T(8,128)(2,1)S(1)} %get-tuple-element.120), kind=kOutput, calls=%fused_computation.6.clone.1 | convolution fusion | flops 806092800 | bytes 4980740 | tf_op jit(solution)/shard_map/while/body/eval_jaxpr/yxz,ysz->xs/dot_general | solution.py:28
  198.3 5.2 %gather_fusion = bf16[12,256,256]{2,1,0:T(8,128)(2,1)S(1)} fusion(bf16[96,256,256]{2,1,0:T(8,128)(2,1)} %get-tuple-element.119, s32[1024]{0:T(1024)S(1)} %pad_clamp_fusion.3), kind=kCustom, calls=%fused_computation.clone.1 | custom fusion | bytes 3145776 | tf_op jit(solution)/shard_map/while/body/eval_jaxpr/gather | solution.py:24
  203.5 3.4 %fusion.27 = f32[6,256,256]{2,1,0:T(8,128)} fusion(f32[6,256,256]{2,1,0:T(8,128)} %get-tuple-element.110, s32[]{:T(128)S(6)} %copy.38, bf16[12,256,256]{2,1,0:T(8,128)(2,1)} %get-tuple-element.121, bf16[12,256,256]{2,1,0:T(8,128)(2,1)S(1)} %gather_fusion, bf16[12,256,256]{2,1,0:T(8,128)(2,1)S(1)} %get-tuple-element.120), kind=kOutput, calls=%fused_computation.6.clone.1 | convolution fusion | flops 806092800 | bytes 4980740 | tf_op jit(solution)/shard_map/while/body/eval_jaxpr/yxz,ysz->xs/dot_general | solution.py:28
  206.9 5.2 %gather_fusion = bf16[12,256,256]{2,1,0:T(8,128)(2,1)S(1)} fusion(bf16[96,256,256]{2,1,0:T(8,128)(2,1)} %get-tuple-element.119, s32[1024]{0:T(1024)S(1)} %pad_clamp_fusion.3), kind=kCustom, calls=%fused_computation.clone.1 | custom fusion | bytes 3145776 | tf_op jit(solution)/shard_map/while/body/eval_jaxpr/gather | solution.py:24
  212.2 3.4 %fusion.27 = f32[6,256,256]{2,1,0:T(8,128)} fusion(f32[6,256,256]{2,1,0:T(8,128)} %get-tuple-element.110, s32[]{:T(128)S(6)} %copy.38, bf16[12,256,256]{2,1,0:T(8,128)(2,1)} %get-tuple-element.121, bf16[12,256,256]{2,1,0:T(8,128)(2,1)S(1)} %gather_fusion, bf16[12,256,256]{2,1,0:T(8,128)(2,1)S(1)} %get-tuple-element.120), kind=kOutput, calls=%fused_computation.6.clone.1 | convolution fusion | flops 806092800 | bytes 4980740 | tf_op jit(solution)/shard_map/while/body/eval_jaxpr/yxz,ysz->xs/dot_general | solution.py:28
  215.6 0.0 copy-start.3
  215.6 0.0 reduce-scatter.2.cloned.1.call-update
  215.6 0.7 dynamic-slice_bitcast_fusion
  216.4 0.0 copy-done
  216.4 0.3 convolution_bitcast_fusion
  216.6 103.1 %psum.7 = f32[4]{0:T(128)S(1)} all-reduce(f32[4]{0:T(128)S(1)} %convolution_bitcast_fusion), channel_id=1, replica_groups=mesh['term'=32,'sector'=16] {'term','sector'}, use_global_device_ids=true, to_apply=%region_3.4 | all-reduce | flops 4 | bytes 32 | tf_op jit(solution)/shard_map/psum | solution.py:44
  319.8 0.0 copy-done.3
  319.8 0.0 copy-start.4
  319.8 0.2 fusion.9
  320.0 0.0 reduce-scatter.2.cloned.1.call-done
  320.0 1.4 bitcast_add_fusion
  321.4 0.0 copy-done.4
  (16 shorter events, 0.1 us)
Async XLA Ops:
  7.2 209.2 %copy-start = (bf16[4,6,8,256]{3,2,1,0:T(8,128)(2,1)S(1)}, bf16[4,6,8,256]{3,2,1,0:T(8,128)(2,1)}, u32[]{:S(2)}) copy-start(bf16[4,6,8,256]{3,2,1,0:T(8,128)(2,1)} %param.14) | copy-start | bytes 294916
  7.2 2.5 copy-start.1
  7.2 156.3 %all-gather.2.cloned.1.call-start = ((), (), s32[]{:S(2)}) async-start(), calls=%async_computation.1 | async-start | bytes 13369344 | tf_op jit(solution)/shard_map/all_gather | solution.py:20
  7.9 312.1 %reduce-scatter.2.cloned.1.call-start = ((), (), s32[]{:S(2)}) async-start(), calls=%async_computation.2 | async-start | bytes 1622016 | tf_op jit(solution)/shard_map/reduce_scatter | solution.py:36
  9.7 153.9 %copy-start.2 = (bf16[12,256,256]{2,1,0:T(8,128)(2,1)S(1)}, bf16[12,256,256]{2,1,0:T(8,128)(2,1)}, u32[]{:S(2)}) copy-start(bf16[12,256,256]{2,1,0:T(8,128)(2,1)} %param.10) | copy-start | bytes 4718596
  215.6 104.2 %copy-start.3 = (f32[4]{0:T(128)S(1)}, f32[4]{0:T(128)}, u32[]{:S(2)}) copy-start(f32[4]{0:T(128)} %param.15) | copy-start | bytes 52
  319.8 1.6 copy-start.4
Sparse Core Ops, SparseCore 0:
  10.1 153.3 all-gather.1
  215.8 97.6 reduce-scatter.1
where the time goes:
time: 329 us; the launch traced here: 328 us
  waiting for transfers between devices  153 us (47%)
  blocking collectives  103 us (31%)
  local copies, waits for them, and re-layouts  34.5 us (10%)
  matrix products  21 us (6%)
  between operations  14.1 us (4%)
    all_gather x1, waiting for transfers between devices, per_device(): store = lax.all_gather(wavefunction, 'sector', axis=0, tiled=True)  152 us
    psum x1, blocking collectives, per_device(): correlations = lax.psum(local_correlation, ('term', 'sector')) / total_cells  103 us
    gather x6, local copies, waits for them, and re-layouts, one_sector(): input_sectors = store[column]  31.3 us
    dot_general x6, matrix products, one_sector(): jnp.einsum('yxz,ysz->xs', partial_contraction, right_operator_blocks, pre...  20.6 us
  transfers between devices with their start and end apart: 2, of which 1 were waited for; matrix products, arithmetic and copies ran while one was open for 1% of the time, Pallas kernels for 0%

commit v1 on v0

--- a/solution.py
+++ b/solution.py
@@ -17,7 +17,9 @@
     block_width = wavefunction.shape[1]
     group_count = fetch_index.shape[2]
     own_requests = fetch_index.reshape(group_count, 1)
-    store = lax.all_gather(wavefunction, "sector", axis=0, tiled=True)
+    store = jnp.concatenate(
+        lax.all_to_all(jnp.stack([wavefunction] * lax.axis_size("sector")), "sector", 0, 0), axis=0
+    )
     lookup = owner_link * sec_dev + own_requests[:, 0][owner_link]
 
     def one_sector(column):

time: 329 us -> 739 us (2.25)
  waiting for transfers between devices: 153 us -> 539 us
  starting transfers between devices: 0.08 us -> 16 us
    all_to_all x0 -> x1, waiting for transfers between devices: none -> 539 us  [per_device(): lax.all_to_all(jnp.stack([wavefunction] * lax.axis_size('sector')), 'sect...]
    all_gather x1 -> x0, waiting for transfers between devices: 152 us -> none  [per_device(): store = lax.all_gather(wavefunction, 'sector', axis=0, tiled=True)]
    all_to_all x0 -> x1, starting transfers between devices: none -> 15.9 us  [per_device(): lax.all_to_all(jnp.stack([wavefunction] * lax.axis_size('sector')), 'sect...]
  transfers between devices with their start and end apart: 2 -> 2, of which waited for: 1 -> 1; matrix products, arithmetic and copies ran while one was open for 1% -> 0% of each run, Pallas kernels for 0% -> 0%
where the time goes in v1:
time: 739 us; the launch traced here: 738 us
  waiting for transfers between devices  539 us (73%)
  blocking collectives  106 us (14%)
  local copies, waits for them, and re-layouts  41.3 us (6%)
  matrix products  19.8 us (3%)
  starting transfers between devices  16 us (2%)
  between operations  14.1 us (2%)
    all_to_all x1, waiting for transfers between devices, per_device(): lax.all_to_all(jnp.stack([wavefunction] * lax.axis_size('sector')), 'sect...  539 us
    psum x1, blocking collectives, per_device(): correlations = lax.psum(local_correlation, ('term', 'sector')) / total_cells  106 us
    gather x6, local copies, waits for them, and re-layouts, one_sector(): input_sectors = store[column]  31.3 us
    dot_general x6, matrix products, one_sector(): jnp.einsum('yxz,ysz->xs', partial_contraction, right_operator_blocks, pre...  19.4 us
    all_to_all x1, starting transfers between devices, per_device(): lax.all_to_all(jnp.stack([wavefunction] * lax.axis_size('sector')), 'sect...  15.9 us
  transfers between devices with their start and end apart: 2, of which 1 were waited for; matrix products, arithmetic and copies ran while one was open for 0% of the time, Pallas kernels for 0%

profile of v1, /device:TPU:1, one launch (start us, length us, event | category | flops | bytes accessed | tf_op | source)
XLA Modules:
  0.0 738.0 jit_solution(8726470107922474157)
XLA Ops:
  7.2 0.0 copy-start
  7.2 7.2 stack.2
  14.4 0.0 copy-start.2
  14.4 15.9 %all-to-all-start = ((bf16[16,6,256,256]{3,2,1,0:T(8,128)(2,1)}), bf16[16,6,256,256]{3,2,1,0:T(8,128)(2,1)}, u32[]{:S(2)}, u32[]{:S(2)}) async-start(bf16[16,6,256,256]{3,2,1,0:T(8,128)(2,1)} %stack.2), calls=%async_computation | async-start | bytes 25165824 | tf_op jit(solution)/shard_map/all_to_all | solution.py:21
  30.3 0.0 copy-start.1
  30.3 0.0 reduce-scatter.2.cloned.1.call-start
  30.4 0.0 copy-done.2
  30.4 0.1 copy.12
  30.5 0.1 copy.13
  30.6 0.1 reshape.48
  30.7 0.3 copy-done.1
  31.0 0.0 copy-start.3
  31.0 1.2 gather_fusion.1
  32.2 0.1 reshape.47
  32.3 0.1 copy.14
  32.4 539.3 %all-to-all-done = bf16[16,6,256,256]{3,2,1,0:T(8,128)(2,1)} async-done(((bf16[16,6,256,256]{3,2,1,0:T(8,128)(2,1)}), bf16[16,6,256,256]{3,2,1,0:T(8,128)(2,1)}, u32[]{:S(2)}, u32[]{:S(2)}) %all-to-all-start) | async-done | bytes 12582944 | tf_op jit(solution)/shard_map/all_to_all | solution.py:21
  571.6 0.0 copy-done.3
  571.6 50.9 %while.10 = (s32[]{:T(128)}, f32[6,256,256]{2,1,0:T(8,128)}, s32[6,12]{1,0:T(8,128)S(1)}, bf16[96,256,256]{2,1,0:T(8,128)(2,1)}, bf16[12,256,256]{2,1,0:T(8,128)...) while((s32[]{:T(128)}, f32[6,256,256]{2,1,0:T(8,128)}, s32[6,12]{1,0:T(8,128)S(1)}, ...), condition=%wide.region_1.2_spmd, body=%wide.region_0.1_spmd.sunk | while | flops 806093888 | bytes 8131345 | solution.py:37
  571.7 5.2 gather_fusion
  576.9 3.2 fusion.27
  580.1 5.2 gather_fusion
  585.4 3.2 fusion.27
  588.6 5.2 gather_fusion
  593.8 3.2 fusion.27
  597.1 5.2 gather_fusion
  602.3 3.2 fusion.27
  605.6 5.2 gather_fusion
  610.8 3.2 fusion.27
  614.0 5.2 gather_fusion
  619.3 3.2 fusion.27
  622.5 0.0 copy-start.4
  622.5 0.0 reduce-scatter.2.cloned.1.call-update
  622.5 0.7 dynamic-slice_bitcast_fusion
  623.3 0.0 copy-done
  623.3 0.3 convolution_bitcast_fusion
  623.5 106.0 %psum.7 = f32[4]{0:T(128)S(1)} all-reduce(f32[4]{0:T(128)S(1)} %convolution_bitcast_fusion), channel_id=1, replica_groups=mesh['term'=32,'sector'=16] {'term','sector'}, use_global_device_ids=true, to_apply=%region_3.4 | all-reduce | flops 4 | bytes 32 | tf_op jit(solution)/shard_map/psum | solution.py:46
  729.5 0.0 copy-done.4
  729.5 0.0 copy-start.5
  729.5 0.2 fusion.9
  729.7 0.0 reduce-scatter.2.cloned.1.call-done
  729.7 1.4 bitcast_add_fusion
  731.1 0.0 copy-done.5
  (17 shorter events, 0.1 us)
Async XLA Ops:
  7.2 616.1 %copy-start = (bf16[4,6,8,256]{3,2,1,0:T(8,128)(2,1)S(1)}, bf16[4,6,8,256]{3,2,1,0:T(8,128)(2,1)}, u32[]{:S(2)}) copy-start(bf16[4,6,8,256]{3,2,1,0:T(8,128)(2,1)} %param.14) | copy-start | bytes 294916
  14.4 16.0 %copy-start.2 = (s32[12,6]{0,1:T(8,128)S(1)}, s32[12,6]{0,1:T(8,128)}, u32[]{:S(2)}) copy-start(s32[12,6]{0,1:T(8,128)} %param.13) | copy-start | bytes 868
  14.4 557.3 %all-to-all-start = ((bf16[16,6,256,256]{3,2,1,0:T(8,128)(2,1)}), bf16[16,6,256,256]{3,2,1,0:T(8,128)(2,1)}, u32[]{:S(2)}, u32[]{:S(2)}) async-start(bf16[16,6,256,256]{3,2,1,0:T(8,128)(2,1)} %stack.2), calls=%async_computation | async-start | bytes 25165824 | tf_op jit(solution)/shard_map/all_to_all | solution.py:21
  30.3 0.7 copy-start.1
  30.3 699.4 %reduce-scatter.2.cloned.1.call-start = ((), (), s32[]{:S(2)}) async-start(), calls=%async_computation.2 | async-start | bytes 1622016 | tf_op jit(solution)/shard_map/reduce_scatter | solution.py:38
  31.0 540.7 %copy-start.3 = (bf16[12,256,256]{2,1,0:T(8,128)(2,1)S(1)}, bf16[12,256,256]{2,1,0:T(8,128)(2,1)}, u32[]{:S(2)}) copy-start(bf16[12,256,256]{2,1,0:T(8,128)(2,1)} %param.10) | copy-start | bytes 4718596
  622.5 107.0 %copy-start.4 = (f32[4]{0:T(128)S(1)}, f32[4]{0:T(128)}, u32[]{:S(2)}) copy-start(f32[4]{0:T(128)} %param.15) | copy-start | bytes 52
  729.5 1.6 copy-start.5
Sparse Core Ops, SparseCore 0:
  622.6 100.3 reduce-scatter.1
